TPU v7x, 32 devices: a whole 2x2x4 slice. The times are simulated.
32 devices in a mesh: groups: 2 (over y), wide: 4 (over z), narrow: 4 (over x, core).
Axes of the slice: x: 2, y: 2, z: 4, core: 2. Of those that a mesh axis runs over, the one named last changes fastest.
Arguments:
- hidden: bfloat16 [1024, 53248], P(('groups', 'narrow'), 'wide'), parts along dimension 0, may hold values from -6 to 6
- down_weight: bfloat16 [53248, 8192], P('wide', 'narrow'), may hold values from -0.02734375 to 0.02734375
Outputs:
- projected: bfloat16 [1024, 8192], P(('groups', 'wide'), 'narrow'), parts along dimension 0
There are 2 independent parts, one for each index of `groups`. A program takes and returns all parts, laid end to end along the dimension named above; an argument that names none is the same for every part. Nothing has to cross between parts.
All inputs are finite; a program needn't handle non-finite values.
Results may differ from a plain program's by a relative error of at most 0.001.
Values may be sent and summed in bfloat16 or wider, within the bound.
A program may use at most 192 MiB of HBM per device.

v0:
```python
import jax
import jax.numpy as jnp
from jax import lax
from jax.sharding import PartitionSpec as P


def gathered_rows(hidden):
    return lax.all_gather(hidden, "narrow", axis=0, tiled=True)


def per_device(hidden, down_weight):
    gathered = gathered_rows(hidden)
    partial_value = jnp.dot(gathered, down_weight, preferred_element_type=jnp.float32)
    sums = lax.psum_scatter(partial_value, "wide", scatter_dimension=0, tiled=True)
    return sums.astype(jnp.bfloat16)


def solution(mesh):
    in_specs = (P(("groups", "narrow"), "wide"), P("wide", "narrow"))
    out_specs = P(("groups", "wide"), "narrow")
    return jax.shard_map(
        per_device, mesh=mesh, in_specs=in_specs, out_specs=out_specs, check_vma=False
    )
```

profile of v0, /device:TPU:28, one launch (start us, length us, event | category | flops | bytes accessed | tf_op | source)
XLA Modules:
  0.0 220.0 jit_solution(3396523551677974770)
XLA Ops:
  6.5 0.0 all-gather.2.cloned.1.call-start
  6.5 0.7 all-gather.2.cloned.1.call-update
  7.3 0.0 reduce-scatter.2.cloned.1.call-start
  7.3 90.6 %all-gather.2.cloned.1.call-done = bf16[512,13312]{1,0:T(8,128)(2,1)} async-done(((bf16[128,13312]{1,0:T(8,128)(2,1)}), bf16[512,13312]{1,0:T(8,128)(2,1)}) %all-gather.2.cloned.1.call-update) | async-done | bytes 13631504 | tf_op jit(solution)/shard_map/all_gather | solution.py:8
  97.9 36.7 %fusion = f32[512,2048]{1,0:T(8,128)} fusion(bf16[512,13312]{1,0:T(8,128)(2,1)} %all-gather.2.cloned.1.call-done, bf16[13312,2048]{1,0:T(8,128)(2,1)} %param.3), kind=kOutput, calls=%fused_computation | convolution fusion | flops 27917287424 | bytes 72351744 | tf_op jit(solution)/shard_map/dot_general | solution.py:13
  134.6 0.0 reduce-scatter.2.cloned.1.call-update
  134.6 76.4 %reduce-scatter.2.cloned.1.call-done = f32[128,2048]{1,0:T(8,128)} async-done(((f32[512,2048]{1,0:T(8,128)}), f32[128,2048]{1,0:T(8,128)}) %reduce-scatter.2.cloned.1.call-update) | async-done | bytes 1048592 | tf_op jit(solution)/shard_map/reduce_scatter | solution.py:14
  211.0 2.1 convert_element_type.3
Async XLA Ops:
  6.5 91.4 %all-gather.2.cloned.1.call-start = ((), (), s32[]{:S(2)}) async-start(), calls=%async_computation.1 | async-start | bytes 17039360 | tf_op jit(solution)/shard_map/all_gather | solution.py:8
  7.3 203.8 %reduce-scatter.2.cloned.1.call-start = ((), (), s32[]{:S(2)}) async-start(), calls=%async_computation.2 | async-start | bytes 5242880 | tf_op jit(solution)/shard_map/reduce_scatter | solution.py:14
Sparse Core Ops, SparseCore 0:
  8.9 88.9 all-gather.1
  134.7 76.2 reduce-scatter.1
where the time goes:
time: 222 us; the launch traced here: 220 us
  waiting for transfers between devices  168 us (76%)
  matrix products  36.7 us (17%)
  between operations  13.4 us (6%)
    all_gather x1, waiting for transfers between devices, gathered_rows(): return lax.all_gather(hidden, 'narrow', axis=0, tiled=True)  90.6 us
    reduce_scatter x1, waiting for transfers between devices, per_device(): lax.psum_scatter(partial_value, 'wide', scatter_dimension=0, tiled=True)  76.4 us
    dot_general x1, matrix products, per_device(): jnp.dot(gathered, down_weight, preferred_element_type=jnp.float32)  36.7 us
  transfers between devices with their start and end apart: 2, of which 2 were waited for; matrix products, arithmetic and copies ran while one was open for 0% of the time, Pallas kernels for 0%

commit v1 on v0

v1 whole, which is shorter than its diff:
```python
import functools

import jax
import jax.numpy as jnp
from jax import lax
from jax.experimental import pallas as pl
from jax.experimental.pallas import tpu as pltpu
from jax.sharding import PartitionSpec as P

MESH = pl.DeviceIdType.MESH
SLICES = 4
PIECES = 4
UNITS = 2 * PIECES


def plain(hidden, down_weight):
    gathered = lax.all_gather(hidden, "narrow", axis=0, tiled=True)
    partial_value = jnp.dot(gathered, down_weight, preferred_element_type=jnp.float32)
    sums = lax.psum_scatter(partial_value, "wide", scatter_dimension=0, tiled=True)
    return sums.astype(jnp.bfloat16)


def turn(chunk, hop, u):
    if chunk == 0:
        return 2 * hop + lax.div(3 * u, 4)
    if chunk == 1:
        return 3 + hop + lax.div(u + 1, 2)
    return 7 + hop + lax.div(u, PIECES)


def kernel(tokens, depth, cols, h_ref, w_ref, out_ref, hv, wv, part, from_left, from_right,
           own_sem, w_sem, sib_send, sib_recv, x_send, x_recv, f_send, f_recv,
           z_send, left_recv, right_recv):
    g, z, n = (lax.axis_index(a) for a in ("groups", "wide", "narrow"))
    core = lax.rem(n, 2)
    sib = n + 1 - 2 * core
    far = lax.rem(n + 2, 4)
    ks = depth // SLICES
    pc = cols // PIECES
    halves = [tokens, tokens // 2, tokens // 4, tokens // 4]
    inner = [0, 0, tokens // 2, 3 * tokens // 4]
    bases = [0, 2 * tokens, 3 * tokens, 3 * tokens + tokens // 2]
    chunks = len(halves)

    barrier = pltpu.get_barrier_semaphore()
    pl.semaphore_signal(barrier, inc=1, device_id=(g, z, sib), device_id_type=MESH)
    pl.semaphore_signal(barrier, inc=1, device_id=(g, z, far), device_id_type=MESH)

    @pl.when(z > 0)
    def _():
        pl.semaphore_signal(barrier, inc=1, device_id=(g, z - 1, n), device_id_type=MESH)

    @pl.when(z < 3)
    def _():
        pl.semaphore_signal(barrier, inc=1, device_id=(g, z + 1, n), device_id_type=MESH)

    def w_copy(t):
        return pltpu.make_async_copy(
            w_ref.at[pl.ds((t % SLICES) * ks, ks)], wv.at[t % 2], w_sem.at[t % 2])

    def own_copy(s):
        k = pl.ds(s * ks, ks)
        return pltpu.make_async_copy(h_ref.at[:, k], hv.at[pl.ds(0, tokens), k], own_sem.at[s])

    def sib_copy(s):
        k = pl.ds(s * ks, ks)
        return pltpu.make_async_remote_copy(
            h_ref.at[:, k], hv.at[pl.ds(tokens, tokens), k], sib_send.at[s], sib_recv.at[s],
            device_id=(g, z, sib), device_id_type=MESH)

    def x_copy(c, s):
        k = pl.ds(s * ks, ks)
        i = (c - 1) * SLICES + s
        return pltpu.make_async_remote_copy(
            h_ref.at[pl.ds(inner[c], halves[c]), k], hv.at[pl.ds(bases[c], halves[c]), k],
            x_send.at[i], x_recv.at[i], device_id=(g, z, far), device_id_type=MESH)

    def f_copy(c, s):
        k = pl.ds(s * ks, ks)
        i = (c - 1) * SLICES + s
        return pltpu.make_async_remote_copy(
            hv.at[pl.ds(bases[c], halves[c]), k],
            hv.at[pl.ds(bases[c] + halves[c], halves[c]), k],
            f_send.at[i], f_recv.at[i], device_id=(g, z, sib), device_id_type=MESH)

    w_copy(0).start()
    own_copy(0).start()
    w_copy(1).start()
    pl.semaphore_wait(barrier, 2 + (z > 0).astype(jnp.int32) + (z < 3).astype(jnp.int32))
    for s in range(SLICES):
        sib_copy(s).start()
        x_copy(1, s).start()
    for s in range(1, SLICES):
        own_copy(s).start()

    def unit(c, u):
        item, piece = lax.div(u, PIECES), lax.rem(u, PIECES)
        rows = pl.ds(pl.multiple_of(bases[c] + item * halves[c], 16), halves[c])
        columns = pl.ds(pl.multiple_of(piece * pc, pc), pc)
        first, second = (n, sib) if c == 0 else (far, lax.rem(sib + 2, 4))
        block = jnp.where(item == 0, first, second)
        return rows, columns, block

    def to_right(c, u):
        rows, columns, _ = unit(c, u)
        return pltpu.make_async_remote_copy(
            part.at[rows, columns], from_left.at[rows, columns],
            z_send.at[c * UNITS + u], left_recv.at[c * UNITS + u],
            device_id=(g, z + 1, n), device_id_type=MESH)

    def to_left(c, u):
        rows, columns, _ = unit(c, u)
        return pltpu.make_async_remote_copy(
            part.at[rows, columns], from_right.at[rows, columns],
            z_send.at[c * UNITS + u], right_recv.at[c * UNITS + u],
            device_id=(g, z - 1, n), device_id_type=MESH)

    def hop_of(block):
        return jnp.where(z < block, z, jnp.where(z > block, 3 - z, jnp.maximum(block, 3 - block)))

    def reduce_unit(c, u):
        rows, columns, block = unit(c, u)

        @pl.when(jnp.logical_and(z > 0, z <= block))
        def _():
            to_right(c, u).wait_recv()
            part[rows, columns] += from_left[rows, columns]

        @pl.when(jnp.logical_and(z < 3, z >= block))
        def _():
            to_left(c, u).wait_recv()
            part[rows, columns] += from_right[rows, columns]

        @pl.when(z < block)
        def _():
            to_right(c, u).start()

        @pl.when(z > block)
        def _():
            to_left(c, u).start()

        @pl.when(z == block)
        def _():
            out_ref[pl.ds(inner[c], halves[c]), columns] = part[rows, columns].astype(out_ref.dtype)

    def reduce_where(c, chosen):
        def body(u, carry):
            hop = hop_of(unit(c, u)[2])

            @pl.when(chosen(hop, u))
            def _():
                reduce_unit(c, u)
            return carry
        lax.fori_loop(0, UNITS, body, 0)

    nt = min(cols, 256)
    for c in range(chunks):
        rows = pl.ds(bases[c], 2 * halves[c])
        for s in range(SLICES):
            t = c * SLICES + s
            k = pl.ds(s * ks, ks)
            if c == 0:
                own_copy(s).wait()
                sib_copy(s).wait_recv()
            else:
                x_copy(c, s).wait_recv()
                f_copy(c, s).start()
                f_copy(c, s).wait_recv()
            w_copy(t).wait()

            def tile(j, carry):
                columns = pl.ds(pl.multiple_of(j * nt, nt), nt)
                product = jnp.dot(hv[rows, k], wv[t % 2, :, columns],
                                  preferred_element_type=jnp.float32)
                if s == 0:
                    part[rows, columns] = product
                else:
                    part[rows, columns] += product
                return carry
            lax.fori_loop(0, cols // nt, tile, 0)
            if t + 2 < chunks * SLICES:
                w_copy(t + 2).start()
            if s == SLICES - 1:
                reduce_where(c, lambda hop, u: hop == 0)
                if c + 2 < chunks:
                    for q in range(SLICES):
                        x_copy(c + 2, q).start()
            if c > 0:
                b = t - SLICES
                for e in range(min(c, chunks - 1)):
                    reduce_where(e, lambda hop, u, e=e: jnp.logical_and(hop > 0, turn(e, hop, u) == b))
    reduce_where(chunks - 1, lambda hop, u: hop > 0)

    for s in range(SLICES):
        sib_copy(s).wait_send()
    for c in range(1, chunks):
        for s in range(SLICES):
            x_copy(c, s).wait_send()
            f_copy(c, s).wait_send()
    for c in range(chunks):
        def done(u, carry):
            block = unit(c, u)[2]

            @pl.when(z != block)
            def _():
                to_right(c, u).wait_send()
            return carry
        lax.fori_loop(0, UNITS, done, 0)


def fused(hidden, down_weight):
    tokens, depth = hidden.shape
    cols = down_weight.shape[1]
    dma = pltpu.SemaphoreType.DMA
    remote = 3 * SLICES
    return pl.pallas_call(
        functools.partial(kernel, tokens, depth, cols),
        out_shape=jax.ShapeDtypeStruct((tokens, cols), jnp.bfloat16),
        in_specs=[pl.BlockSpec(memory_space=pl.ANY)] * 2,
        out_specs=pl.BlockSpec(memory_space=pltpu.VMEM),
        scratch_shapes=[
            pltpu.VMEM((4 * tokens, depth), jnp.bfloat16),
            pltpu.VMEM((2, depth // SLICES, cols), jnp.bfloat16),
            pltpu.VMEM((4 * tokens, cols), jnp.float32),
            pltpu.VMEM((4 * tokens, cols), jnp.float32),
            pltpu.VMEM((4 * tokens, cols), jnp.float32),
            dma((SLICES,)), dma((2,)), dma((SLICES,)), dma((SLICES,)),
            dma((remote,)), dma((remote,)), dma((remote,)), dma((remote,)),
            dma((4 * UNITS,)), dma((4 * UNITS,)), dma((4 * UNITS,)),
        ],
        compiler_params=pltpu.CompilerParams(
            collective_id=0, has_side_effects=True, vmem_limit_bytes=60 << 20),
        cost_estimate=pl.CostEstimate(
            flops=8 * tokens * depth * cols, bytes_accessed=8 * depth * cols, transcendentals=0),
    )(hidden, down_weight)


def solution(mesh):
    def per_device(hidden, down_weight):
        fits = (mesh.shape["narrow"] == 4 and mesh.shape["wide"] == 4
                and hidden.shape[0] == 128 and hidden.shape[1] % (SLICES * 256) == 0
                and hidden.shape[1] <= 13312 and down_weight.shape[1] % 512 == 0
                and down_weight.shape[1] <= 2048)
        return (fused if fits else plain)(hidden, down_weight)

    in_specs = (P(("groups", "narrow"), "wide"), P("wide", "narrow"))
    out_specs = P(("groups", "wide"), "narrow")
    return jax.shard_map(
        per_device, mesh=mesh, in_specs=in_specs, out_specs=out_specs, check_vma=False
    )
```

time: 222 us -> 127 us (0.57)
  waiting for transfers between devices: 168 us -> 0 us
  Pallas kernels: 0 us -> 124 us
  matrix products: 36.7 us -> 0 us
  between operations: 13.4 us -> 0.01 us
    pallas_call x0 -> x1, Pallas kernels: none -> 124 us  [fused(): pl.pallas_call(functools.partial(kernel, tokens, depth, cols), out_shape=...]
    all_gather x1 -> x0, waiting for transfers between devices: 90.6 us -> none  [gathered_rows(): return lax.all_gather(hidden, 'narrow', axis=0, tiled=True)]
    reduce_scatter x1 -> x0, waiting for transfers between devices: 76.4 us -> none  [per_device(): lax.psum_scatter(partial_value, 'wide', scatter_dimension=0, tiled=True)]
    dot_general x1 -> x0, matrix products: 36.7 us -> none  [per_device(): jnp.dot(gathered, down_weight, preferred_element_type=jnp.float32)]
  transfers between devices with their start and end apart: 2 -> 0, of which waited for: 2 -> 0; matrix products, arithmetic and copies ran while one was open for 0% -> 0% of each run, Pallas kernels for 0% -> 0%
where the time goes in v1:
time: 127 us; the launch traced here: 126 us
  Pallas kernels  124 us (98%)
  local copies, waits for them, and re-layouts  1.88 us (1%)
    pallas_call x1, Pallas kernels, fused(): pl.pallas_call(functools.partial(kernel, tokens, depth, cols), out_shape=...  124 us

profile of v1, /device:TPU:28, one launch (start us, length us, event | category | flops | bytes accessed | tf_op | source)
XLA Modules:
  0.0 126.4 jit_solution(6689707679940469320)
XLA Ops:
  0.0 124.5 %shard_map.28 = bf16[128,2048]{1,0:T(8,128)(2,1)} custom-call(bf16[128,13312]{1,0:T(8,128)(2,1)} %h_ref.1, bf16[13312,2048]{1,0:T(8,128)(2,1)} %w_ref.1), custom_call_target="tpu_custom_call" | custom-call | flops 27917287424 | bytes 218103808 | tf_op jit(solution)/shard_map/pallas_call | solution.py:216
  124.5 1.9 %copy.4 = bf16[128,2048]{1,0:T(8,128)(2,1)} copy(bf16[128,2048]{1,0:T(8,128)(2,1)} %shard_map.28) | data formatting | bytes 1048576

commit v2 on v1

--- a/solution.py
+++ b/solution.py
@@ -26,6 +26,11 @@
     if chunk == 1:
         return 3 + hop + lax.div(u + 1, 2)
     return 7 + hop + lax.div(u, PIECES)
+
+
+def slice_order(chunk):
+    order = list(range(SLICES))
+    return order if chunk % 2 == 0 else order[::-1]
 
 
 def kernel(tokens, depth, cols, h_ref, w_ref, out_ref, hv, wv, part, from_left, from_right,
@@ -37,9 +42,9 @@
     far = lax.rem(n + 2, 4)
     ks = depth // SLICES
     pc = cols // PIECES
-    halves = [tokens, tokens // 2, tokens // 4, tokens // 4]
-    inner = [0, 0, tokens // 2, 3 * tokens // 4]
-    bases = [0, 2 * tokens, 3 * tokens, 3 * tokens + tokens // 2]
+    halves = [tokens, tokens // 2, 3 * tokens // 8, tokens // 8]
+    inner = [0, 0, tokens // 2, 7 * tokens // 8]
+    bases = [0, 2 * tokens, 3 * tokens, 3 * tokens + 3 * tokens // 4]
     chunks = len(halves)
 
     barrier = pltpu.get_barrier_semaphore()
@@ -56,7 +61,7 @@
 
     def w_copy(t):
         return pltpu.make_async_copy(
-            w_ref.at[pl.ds((t % SLICES) * ks, ks)], wv.at[t % 2], w_sem.at[t % 2])
+            w_ref.at[pl.ds(t * ks, ks)], wv.at[t % 2], w_sem.at[t % 2])
 
     def own_copy(s):
         k = pl.ds(s * ks, ks)
@@ -89,7 +94,7 @@
     pl.semaphore_wait(barrier, 2 + (z > 0).astype(jnp.int32) + (z < 3).astype(jnp.int32))
     for s in range(SLICES):
         sib_copy(s).start()
-        x_copy(1, s).start()
+        x_copy(1, SLICES - 1 - s).start()
     for s in range(1, SLICES):
         own_copy(s).start()
 
@@ -156,8 +161,9 @@
     nt = min(cols, 256)
     for c in range(chunks):
         rows = pl.ds(bases[c], 2 * halves[c])
-        for s in range(SLICES):
-            t = c * SLICES + s
+        order = slice_order(c)
+        for i, s in enumerate(order):
+            t = c * SLICES + i
             k = pl.ds(s * ks, ks)
             if c == 0:
                 own_copy(s).wait()
@@ -166,24 +172,25 @@
                 x_copy(c, s).wait_recv()
                 f_copy(c, s).start()
                 f_copy(c, s).wait_recv()
-            w_copy(t).wait()
+            if c == 0 or i >= 2:
+                w_copy(s).wait()
 
             def tile(j, carry):
                 columns = pl.ds(pl.multiple_of(j * nt, nt), nt)
-                product = jnp.dot(hv[rows, k], wv[t % 2, :, columns],
+                product = jnp.dot(hv[rows, k], wv[s % 2, :, columns],
                                   preferred_element_type=jnp.float32)
-                if s == 0:
+                if i == 0:
                     part[rows, columns] = product
                 else:
                     part[rows, columns] += product
                 return carry
             lax.fori_loop(0, cols // nt, tile, 0)
-            if t + 2 < chunks * SLICES:
-                w_copy(t + 2).start()
-            if s == SLICES - 1:
+            if i + 2 < SLICES:
+                w_copy(order[i + 2]).start()
+            if i == SLICES - 1:
                 reduce_where(c, lambda hop, u: hop == 0)
                 if c + 2 < chunks:
-                    for q in range(SLICES):
+                    for q in slice_order(c + 2):
                         x_copy(c + 2, q).start()
             if c > 0:
                 b = t - SLICES

time: 127 us -> 124 us (0.976)
  Pallas kernels: 124 us -> 122 us
    pallas_call x1, Pallas kernels: 124 us -> 122 us  [fused(): pl.pallas_call(functools.partial(kernel, tokens, depth, cols), out_shape=...]
where the time goes in v2:
time: 124 us
  Pallas kernels  122 us (98%)
  local copies, waits for them, and re-layouts  1.88 us (2%)
    pallas_call x1, Pallas kernels, fused(): pl.pallas_call(functools.partial(kernel, tokens, depth, cols), out_shape=...  122 us

profile of v2, /device:TPU:28, one launch (start us, length us, event | category | flops | bytes accessed | tf_op | source)
XLA Modules:
  0.0 123.6 jit_solution(2697574432917374182)
XLA Ops:
  0.0 121.7 %shard_map.28 = bf16[128,2048]{1,0:T(8,128)(2,1)} custom-call(bf16[128,13312]{1,0:T(8,128)(2,1)} %h_ref.1, bf16[13312,2048]{1,0:T(8,128)(2,1)} %w_ref.1), custom_call_target="tpu_custom_call" | custom-call | flops 27917287424 | bytes 218103808 | tf_op jit(solution)/shard_map/pallas_call | solution.py:223
  121.7 1.9 %copy.4 = bf16[128,2048]{1,0:T(8,128)(2,1)} copy(bf16[128,2048]{1,0:T(8,128)(2,1)} %shard_map.28) | data formatting | bytes 1048576
